TPU v7x, 32 devices: a whole 2x2x4 slice. The times are simulated.
32 devices in a mesh: ctx: 16 (over z, y, core), head: 2 (over x).
Axes of the slice: x: 2, y: 2, z: 4, core: 2. Of those that a mesh axis runs over, the one named last changes fastest.
Arguments:
- queries: bfloat16 [16384, 4096], P('ctx', 'head'), may hold values from -10 to 10, as said below
- keys: bfloat16 [16384, 4096], P('ctx', 'head'), may hold values from -4.6 to 4.6, as said below
- values: bfloat16 [16384, 4096], P('ctx', 'head'), may hold values from -6 to 6
Outputs:
- attended: bfloat16 [16384, 4096], P('ctx', 'head')
Inputs may be any that keep to these rules, and one draw needn't show every extreme that they name: real-valued queries. real-valued keys.
All inputs are finite; a program needn't handle non-finite values.
Results may differ from a plain program's by a relative error of at most 0.0099.
Values may be sent and summed in bfloat16 or wider, within the bound.
A program may use at most 128 MiB of HBM per device.

v0:
```python
import jax
import jax.numpy as jnp
from jax import lax
from jax.sharding import PartitionSpec as P

HD = 128
POOL = 256
EDGE = 256


def extended(value, sides, width):
    for axis, dim in sides:
        size, length = (lax.axis_size(axis), value.shape[dim])
        up = [(i, (i + 1) % size) for i in range(size - 1)]
        down = [(j, i) for i, j in up]
        last = lax.slice_in_dim(value, length - width, length, axis=dim)
        leading = lax.slice_in_dim(value, 0, width, axis=dim)
        before = lax.ppermute(last, axis, up)
        after = lax.ppermute(leading, axis, down)
        value = jnp.concatenate([before, value, after], axis=dim)
    return value


def from_partner(value, axis, apart):
    mask = 2**apart
    pairs = [(source, source ^ mask) for source in range(lax.axis_size(axis))]
    return lax.ppermute(value, axis, pairs)


def pool_rows(block, group):
    shape = block.shape
    grouped = block.reshape(shape[:-2] + (shape[-2] // group, group, shape[-1])).astype(jnp.float32)
    return (jnp.sum(grouped, axis=-2) / jnp.float32(group**0.5)).astype(jnp.bfloat16)


def on_device(queries, keys, values):
    tok_rows, width = queries.shape
    heads_dev = width // HD
    count = lax.axis_size("ctx")
    depth_count = count.bit_length() - 1
    position = lax.axis_index("ctx")
    scale = jnp.float32(HD ** (-0.5))
    paired = jnp.stack((keys, values))
    level = pool_rows(paired, tok_rows // POOL)
    siblings = []
    partner = level
    padded = extended(paired, (("ctx", 1),), EDGE)
    left = padded[:, :EDGE]
    right = padded[:, EDGE + tok_rows :]
    for depth in range(depth_count):
        partner = from_partner(level, "ctx", depth)
        siblings.append(partner)
        if depth + 1 < depth_count:
            upper_half = position // 2**depth % 2 == 1
            lower = jnp.where(upper_half, partner, level)
            upper = jnp.where(upper_half, level, partner)
            level = pool_rows(jnp.concatenate([lower, upper], axis=1), 2)
    key_set = jnp.concatenate([paired, left, right] + siblings, axis=1)
    total = key_set.shape[1]
    valid = jnp.concatenate(
        [
            jnp.ones((tok_rows,), bool),
            jnp.broadcast_to(position > 0, (EDGE,)),
            jnp.broadcast_to(position < count - 1, (EDGE,)),
            jnp.ones((total - tok_rows - 2 * EDGE,), bool),
        ]
    )
    block_rows = min(512, tok_rows)
    block_count = tok_rows // block_rows

    def one_head(head_index):
        key_head = lax.dynamic_slice_in_dim(key_set[0], head_index * HD, HD, 1)
        value_head = lax.dynamic_slice_in_dim(key_set[1], head_index * HD, HD, 1)
        query_head = lax.dynamic_slice_in_dim(queries, head_index * HD, HD, 1)

        def one_block(block_index):
            query = lax.dynamic_slice_in_dim(query_head, block_index * block_rows, block_rows, 0)
            scores = (
                lax.dot_general(
                    query, key_head, (((1,), (1,)), ((), ())), preferred_element_type=jnp.float32
                )
                * scale
            )
            scores = jnp.where(valid[None, :], scores, jnp.float32(-1e30))
            peak = jnp.max(scores, axis=-1, keepdims=True)
            probs = jnp.exp(scores - peak)
            denom = jnp.sum(probs, axis=-1)
            weights = probs.astype(jnp.bfloat16)
            numer = jnp.dot(weights, value_head, preferred_element_type=jnp.float32)
            return (numer / denom[:, None]).astype(jnp.bfloat16)

        blocks = lax.map(one_block, jnp.arange(block_count, dtype=jnp.int32))
        return blocks.reshape(tok_rows, HD)

    per_head = lax.map(one_head, jnp.arange(heads_dev, dtype=jnp.int32))
    return jnp.transpose(per_head, (1, 0, 2)).reshape(tok_rows, width)


def solution(mesh):
    return jax.shard_map(
        on_device,
        mesh=mesh,
        in_specs=(P("ctx", "head"), P("ctx", "head"), P("ctx", "head")),
        out_specs=P("ctx", "head"),
        check_vma=False,
    )
```

profile of v0, /device:TPU:0, one launch (start us, length us, event | category | flops | bytes accessed | tf_op | source)
XLA Modules:
  0.0 681.8 jit_solution(17520474697638048225)
XLA Ops:
  23.0 12.9 %convert_reduce_fusion = f32[2,256,2048]{2,1,0:T(8,128)S(1)} fusion(bf16[1,256,4,2048]{3,2,1,0:T(4,128)(2,1)} %stack.19, bf16[1,256,4,2048]{3,2,1,0:T(4,128)(2,1)} %stack.18), kind=kLoop, calls=%fused_computation.16 | loop fusion | flops 11534336 | bytes 12582912 | tf_op jit(solution)/shard_map/reduce_sum | solution.py:33
  63.6 10.6 %reshape.29 = f32[2,256,2,2048]{3,2,1,0:T(2,128)} reshape(f32[2,512,2048]{2,1,0:T(8,128)} %maximum_convert_fusion) | data formatting | bytes 16777216 | tf_op jit(solution)/shard_map/convert_element_type | solution.py:32
  74.2 13.3 %reduce_sum.46 = f32[2,256,2048]{2,1,0:T(8,128)} reduce(f32[2,256,2,2048]{3,2,1,0:T(2,128)} %reshape.29, f32[]{:T(128)} %constant.101.clone.1), dimensions={2}, to_apply=%region_1.2 | reduce | flops 1048576 | bytes 12582916 | tf_op jit(solution)/shard_map/reduce_sum | solution.py:33
  97.8 45.4 %collective-permute-done.3 = bf16[2,256,2048]{2,1,0:T(8,128)(2,1)S(1)} collective-permute-done((bf16[2,256,2048]{2,1,0:T(8,128)(2,1)}, bf16[2,256,2048]{2,1,0:T(8,128)(2,1)S(1)}, u32[]{:S(2)}, u32[]{:S(2)}) %collective-permute-start.3) | collective-permute-done | bytes 2097184 | tf_op jit(solution)/shard_map/ppermute | solution.py:27
  152.3 10.6 %reshape.30 = f32[2,256,2,2048]{3,2,1,0:T(2,128)} reshape(f32[2,512,2048]{2,1,0:T(8,128)} %maximum_convert_fusion.1) | data formatting | bytes 16777216 | tf_op jit(solution)/shard_map/convert_element_type | solution.py:32
  162.8 13.5 %reduce_sum.47 = f32[2,256,2048]{2,1,0:T(8,128)} reduce(f32[2,256,2,2048]{3,2,1,0:T(2,128)} %reshape.30, f32[]{:T(128)} %constant.101.clone.1), dimensions={2}, to_apply=%region_2.3 | reduce | flops 1048576 | bytes 12582916 | tf_op jit(solution)/shard_map/reduce_sum | solution.py:33
  181.9 44.9 %collective-permute-done.4 = bf16[2,256,2048]{2,1,0:T(8,128)(2,1)S(1)} collective-permute-done((bf16[2,256,2048]{2,1,0:T(8,128)(2,1)}, bf16[2,256,2048]{2,1,0:T(8,128)(2,1)S(1)}, u32[]{:S(2)}, u32[]{:S(2)}) %collective-permute-start.4) | collective-permute-done | bytes 2097184 | tf_op jit(solution)/shard_map/ppermute | solution.py:27
  235.9 10.6 %reshape.31 = f32[2,256,2,2048]{3,2,1,0:T(2,128)} reshape(f32[2,512,2048]{2,1,0:T(8,128)} %maximum_convert_fusion.2) | data formatting | bytes 16777216 | tf_op jit(solution)/shard_map/convert_element_type | solution.py:32
  246.5 13.3 %reduce_sum.48 = f32[2,256,2048]{2,1,0:T(8,128)} reduce(f32[2,256,2,2048]{3,2,1,0:T(2,128)} %reshape.31, f32[]{:T(128)} %constant.101.clone.1), dimensions={2}, to_apply=%region_3.4 | reduce | flops 1048576 | bytes 12582916 | tf_op jit(solution)/shard_map/reduce_sum | solution.py:33
  265.2 88.7 %collective-permute-done.5 = bf16[2,256,2048]{2,1,0:T(8,128)(2,1)} collective-permute-done((bf16[2,256,2048]{2,1,0:T(8,128)(2,1)S(1)}, bf16[2,256,2048]{2,1,0:T(8,128)(2,1)}, u32[]{:S(2)}, u32[]{:S(2)}) %collective-permute-start.5) | collective-permute-done | bytes 2097184 | tf_op jit(solution)/shard_map/ppermute | solution.py:27
  357.1 319.9 %while.21 = (s32[]{:T(128)}, bf16[16,1024,128]{2,1,0:T(8,128)(2,1)}, s32[16]{0:T(128)S(1)}, bf16[1024,2048]{1,0:T(8,128)(2,1)}, bf16[2,2560,2048]{2,1,0:T(8,128)...) while((s32[]{:T(128)}, ...), condition=%wide.region_9.10_spmd, body=%wide.region_4.9_spmd.sunk | while | flops 680393728 | bytes 62928860 | solution.py:95
  358.3 8.5 %fusion.34 = (bf16[1,2560,2048]{2,1,0:T(8,128)(2,1)S(1)}, bf16[1,2560,2048]{2,1,0:T(8,128)(2,1)S(1)}) fusion(bf16[2,2560,2048]{2,1,0:T(8,128)(2,1)} %get-tuple-element.292), kind=kLoop, calls=%fused_computation.47.clone.1 | loop fusion | bytes 41943040 | tf_op jit(solution)/shard_map/while/body/eval_jaxpr/slice | solution.py:73
  378.3 8.5 %fusion.34 = (bf16[1,2560,2048]{2,1,0:T(8,128)(2,1)S(1)}, bf16[1,2560,2048]{2,1,0:T(8,128)(2,1)S(1)}) fusion(bf16[2,2560,2048]{2,1,0:T(8,128)(2,1)} %get-tuple-element.292), kind=kLoop, calls=%fused_computation.47.clone.1 | loop fusion | bytes 41943040 | tf_op jit(solution)/shard_map/while/body/eval_jaxpr/slice | solution.py:73
  438.3 8.5 %fusion.34 = (bf16[1,2560,2048]{2,1,0:T(8,128)(2,1)S(1)}, bf16[1,2560,2048]{2,1,0:T(8,128)(2,1)S(1)}) fusion(bf16[2,2560,2048]{2,1,0:T(8,128)(2,1)} %get-tuple-element.292), kind=kLoop, calls=%fused_computation.47.clone.1 | loop fusion | bytes 41943040 | tf_op jit(solution)/shard_map/while/body/eval_jaxpr/slice | solution.py:73
  458.3 8.5 %fusion.34 = (bf16[1,2560,2048]{2,1,0:T(8,128)(2,1)S(1)}, bf16[1,2560,2048]{2,1,0:T(8,128)(2,1)S(1)}) fusion(bf16[2,2560,2048]{2,1,0:T(8,128)(2,1)} %get-tuple-element.292), kind=kLoop, calls=%fused_computation.47.clone.1 | loop fusion | bytes 41943040 | tf_op jit(solution)/shard_map/while/body/eval_jaxpr/slice | solution.py:73
  478.3 8.5 %fusion.34 = (bf16[1,2560,2048]{2,1,0:T(8,128)(2,1)S(1)}, bf16[1,2560,2048]{2,1,0:T(8,128)(2,1)S(1)}) fusion(bf16[2,2560,2048]{2,1,0:T(8,128)(2,1)} %get-tuple-element.292), kind=kLoop, calls=%fused_computation.47.clone.1 | loop fusion | bytes 41943040 | tf_op jit(solution)/shard_map/while/body/eval_jaxpr/slice | solution.py:73
  498.2 8.5 %fusion.34 = (bf16[1,2560,2048]{2,1,0:T(8,128)(2,1)S(1)}, bf16[1,2560,2048]{2,1,0:T(8,128)(2,1)S(1)}) fusion(bf16[2,2560,2048]{2,1,0:T(8,128)(2,1)} %get-tuple-element.292), kind=kLoop, calls=%fused_computation.47.clone.1 | loop fusion | bytes 41943040 | tf_op jit(solution)/shard_map/while/body/eval_jaxpr/slice | solution.py:73
  518.2 8.5 %fusion.34 = (bf16[1,2560,2048]{2,1,0:T(8,128)(2,1)S(1)}, bf16[1,2560,2048]{2,1,0:T(8,128)(2,1)S(1)}) fusion(bf16[2,2560,2048]{2,1,0:T(8,128)(2,1)} %get-tuple-element.292), kind=kLoop, calls=%fused_computation.47.clone.1 | loop fusion | bytes 41943040 | tf_op jit(solution)/shard_map/while/body/eval_jaxpr/slice | solution.py:73
  538.2 8.5 %fusion.34 = (bf16[1,2560,2048]{2,1,0:T(8,128)(2,1)S(1)}, bf16[1,2560,2048]{2,1,0:T(8,128)(2,1)S(1)}) fusion(bf16[2,2560,2048]{2,1,0:T(8,128)(2,1)} %get-tuple-element.292), kind=kLoop, calls=%fused_computation.47.clone.1 | loop fusion | bytes 41943040 | tf_op jit(solution)/shard_map/while/body/eval_jaxpr/slice | solution.py:73
  558.2 8.5 %fusion.34 = (bf16[1,2560,2048]{2,1,0:T(8,128)(2,1)S(1)}, bf16[1,2560,2048]{2,1,0:T(8,128)(2,1)S(1)}) fusion(bf16[2,2560,2048]{2,1,0:T(8,128)(2,1)} %get-tuple-element.292), kind=kLoop, calls=%fused_computation.47.clone.1 | loop fusion | bytes 41943040 | tf_op jit(solution)/shard_map/while/body/eval_jaxpr/slice | solution.py:73
  578.2 8.5 %fusion.34 = (bf16[1,2560,2048]{2,1,0:T(8,128)(2,1)S(1)}, bf16[1,2560,2048]{2,1,0:T(8,128)(2,1)S(1)}) fusion(bf16[2,2560,2048]{2,1,0:T(8,128)(2,1)} %get-tuple-element.292), kind=kLoop, calls=%fused_computation.47.clone.1 | loop fusion | bytes 41943040 | tf_op jit(solution)/shard_map/while/body/eval_jaxpr/slice | solution.py:73
  598.2 8.5 %fusion.34 = (bf16[1,2560,2048]{2,1,0:T(8,128)(2,1)S(1)}, bf16[1,2560,2048]{2,1,0:T(8,128)(2,1)S(1)}) fusion(bf16[2,2560,2048]{2,1,0:T(8,128)(2,1)} %get-tuple-element.292), kind=kLoop, calls=%fused_computation.47.clone.1 | loop fusion | bytes 41943040 | tf_op jit(solution)/shard_map/while/body/eval_jaxpr/slice | solution.py:73
  618.2 8.5 %fusion.34 = (bf16[1,2560,2048]{2,1,0:T(8,128)(2,1)S(1)}, bf16[1,2560,2048]{2,1,0:T(8,128)(2,1)S(1)}) fusion(bf16[2,2560,2048]{2,1,0:T(8,128)(2,1)} %get-tuple-element.292), kind=kLoop, calls=%fused_computation.47.clone.1 | loop fusion | bytes 41943040 | tf_op jit(solution)/shard_map/while/body/eval_jaxpr/slice | solution.py:73
  638.2 8.5 %fusion.34 = (bf16[1,2560,2048]{2,1,0:T(8,128)(2,1)S(1)}, bf16[1,2560,2048]{2,1,0:T(8,128)(2,1)S(1)}) fusion(bf16[2,2560,2048]{2,1,0:T(8,128)(2,1)} %get-tuple-element.292), kind=kLoop, calls=%fused_computation.47.clone.1 | loop fusion | bytes 41943040 | tf_op jit(solution)/shard_map/while/body/eval_jaxpr/slice | solution.py:73
  (280 shorter events, 404.8 us)
Async XLA Ops:
  3.7 46.6 %collective-permute-start = (bf16[2,256,2048]{2,1,0:T(8,128)(2,1)}, bf16[2,256,2048]{2,1,0:T(8,128)(2,1)}, u32[]{:S(2)}, u32[]{:S(2)}) collective-permute-start(bf16[2,256,2048]{2,1,0:T(8,128)(2,1)} %get-tuple-element.108), channel_id=1, source_target_pairs={{0,2},{2,4},{4,6},{6,8},{8,10},{10,12},{12,14},{14,16},{16,18},{18... | collective-permute-start | bytes 6291464 | tf_op jit(solution)/shard_map/ppermute | solution.py:18
  7.4 46.2 %collective-permute-start.1 = (bf16[2,256,2048]{2,1,0:T(8,128)(2,1)}, bf16[2,256,2048]{2,1,0:T(8,128)(2,1)}, u32[]{:S(2)}, u32[]{:S(2)}) collective-permute-start(bf16[2,256,2048]{2,1,0:T(8,128)(2,1)} %get-tuple-element.107), channel_id=1, source_target_pairs={{2,0},{4,2},{6,4},{8,6},{10,8},{12,10},{14,12},{16,14},{18,16},{20... | collective-permute-start | bytes 6291464 | tf_op jit(solution)/shard_map/ppermute | solution.py:19
  36.0 2.0 copy-start
  39.9 16.9 %collective-permute-start.2 = (bf16[2,256,2048]{2,1,0:T(8,128)(2,1)}, bf16[2,256,2048]{2,1,0:T(8,128)(2,1)S(1)}, u32[]{:S(2)}, u32[]{:S(2)}) collective-permute-start(bf16[2,256,2048]{2,1,0:T(8,128)(2,1)} %multiply_convert_fusion.3), channel_id=1, source_target_pairs={{0,2},{2,0},{4,6},{6,4},{8,10},{10,8},{12,14},{14,12},{16,18},{18,... | collective-permute-start | bytes 6291464 | tf_op jit(solution)/shard_map/ppermute | solution.py:27
  50.3 6.5 copy-start.1
  91.5 51.7 %collective-permute-start.3 = (bf16[2,256,2048]{2,1,0:T(8,128)(2,1)}, bf16[2,256,2048]{2,1,0:T(8,128)(2,1)S(1)}, u32[]{:S(2)}, u32[]{:S(2)}) collective-permute-start(bf16[2,256,2048]{2,1,0:T(8,128)(2,1)} %multiply_convert_fusion.2), channel_id=1, source_target_pairs={{0,4},{2,6},{4,0},{6,2},{8,12},{10,14},{12,8},{14,10},{16,20},{18,... | collective-permute-start | bytes 6291464 | tf_op jit(solution)/shard_map/ppermute | solution.py:27
  180.4 46.5 %collective-permute-start.4 = (bf16[2,256,2048]{2,1,0:T(8,128)(2,1)}, bf16[2,256,2048]{2,1,0:T(8,128)(2,1)S(1)}, u32[]{:S(2)}, u32[]{:S(2)}) collective-permute-start(bf16[2,256,2048]{2,1,0:T(8,128)(2,1)} %multiply_convert_fusion.1), channel_id=1, source_target_pairs={{0,8},{2,10},{4,12},{6,14},{8,0},{10,2},{12,4},{14,6},{16,24},{18,... | collective-permute-start | bytes 6291464 | tf_op jit(solution)/shard_map/ppermute | solution.py:27
  262.5 91.4 %collective-permute-start.5 = (bf16[2,256,2048]{2,1,0:T(8,128)(2,1)S(1)}, bf16[2,256,2048]{2,1,0:T(8,128)(2,1)}, u32[]{:S(2)}, u32[]{:S(2)}) collective-permute-start(bf16[2,256,2048]{2,1,0:T(8,128)(2,1)S(1)} %multiply_convert_fusion), channel_id=1, source_target_pairs={{0,16},{2,18},{4,20},{6,22},{8,24},{10,26},{12,28},{14,30},{16,0},... | collective-permute-start | bytes 6291464 | tf_op jit(solution)/shard_map/ppermute | solution.py:27
where the time goes:
time: 685 us; the launch traced here: 682 us
  local copies, waits for them, and re-layouts  261 us (38%)
  waiting for transfers between devices  179 us (26%)
  other arithmetic  130 us (19%)
  matrix products  62.8 us (9%)
  loops' own time  31.7 us (5%)
  starting transfers between devices  17.5 us (3%)
    ppermute x4, waiting for transfers between devices, from_partner(): return lax.ppermute(value, axis, pairs)  179 us
    slice x16, local copies, waits for them, and re-layouts, one_head(): value_head = lax.dynamic_slice_in_dim(key_set[1], head_index * HD, HD, 1)  137 us
    reduce_sum x4, other arithmetic, pool_rows(): jnp.sum(grouped, axis=-2) / jnp.float32(group ** 0.5)  53 us
    dot_general x32, matrix products, one_block(): lax.dot_general(query, key_head, (((1,), (1,)), ((), ())), preferred_elem...  32 us
    convert_element_type x3, local copies, waits for them, and re-layouts, pool_rows(): block.reshape(shape[:-2] + (shape[-2] // group, group, shape[-1]))  31.8 us
    dot_general x32, matrix products, one_block(): numer = jnp.dot(weights, value_head, preferred_element_type=jnp.float32)  30.8 us
    reduce_sum x32, other arithmetic, one_block(): denom = jnp.sum(probs, axis=-1)  27 us
    another operation x16, loops' own time, one_head(): blocks = lax.map(one_block, jnp.arange(block_count, dtype=jnp.int32))  20.8 us
  transfers between devices with their start and end apart: 6, of which 3 were waited for; matrix products, arithmetic and copies ran while one was open for 6% of the time, Pallas kernels for 0%

commit v1 on v0

v1 whole, which is shorter than its diff:
```python
import functools
import math

import jax
import jax.numpy as jnp
from jax import lax
from jax.experimental import pallas as pl
from jax.experimental.pallas import tpu as pltpu
from jax.sharding import PartitionSpec as P

HD = 128
POOL = 256
EDGE = 256
SCALE2 = math.log2(math.e) * HD**-0.5
F32 = jnp.float32
BF16 = jnp.bfloat16


def stage_body(kinds, sizes, has_state, final, q_rows, key_cols, *refs):
    flags, q_ref = refs[:2]
    at = 2
    pieces = []
    for _ in kinds:
        pieces.append((refs[at], refs[at + 1]))
        at += 2
    state_ref = None
    if has_state:
        state_ref = refs[at]
        at += 1
    out_ref, k_all, v_all, s_all = refs[at : at + 4]
    total = sum(sizes)
    v_all[:, HD:] = jnp.ones((total, HD), BF16)
    start = 0
    spans = []
    swapped = flags[0] == 1
    for kind, size, (first, second) in zip(kinds, sizes, pieces):
        if kind == "level":
            mine, other = first[...], second[...]
            k_all[start : start + size, :] = jnp.where(swapped, other, mine)
            v_all[start : start + size, :HD] = jnp.where(swapped, mine, other)
        else:
            k_all[start : start + size, :] = first[...]
            v_all[start : start + size, :HD] = second[...]
        flag = {"left": 1, "right": 2}.get(kind)
        step = min(key_cols, size)
        for c in range(start, start + size, step):
            spans.append((c, step, flag))
        start += size
    rows = q_ref.shape[0]
    for r0 in range(0, rows, q_rows):
        q = q_ref[r0 : r0 + q_rows, :]
        slot = (r0 // q_rows) % 2
        peak = None
        for c, width, flag in spans:
            s = lax.dot_general(
                q, k_all[c : c + width, :], (((1,), (1,)), ((), ())), preferred_element_type=F32
            )
            if flag is not None:
                s = jnp.where(flags[flag] == 1, s, F32(-1e30))
            s_all[slot, :, c : c + width] = s
            for j in range(0, width, HD):
                part = s[:, j : j + HD]
                peak = part if peak is None else jnp.maximum(peak, part)
        peak = jnp.max(peak, axis=-1, keepdims=True)
        if has_state:
            before = state_ref[r0 : r0 + q_rows, :]
            old = before[:, 2 * HD - 1 :]
            peak = jnp.maximum(peak, old)
        acc = None
        for c, width, flag in spans:
            p = jnp.exp2((s_all[slot, :, c : c + width] - peak) * F32(SCALE2)).astype(BF16)
            term = jnp.dot(p, v_all[c : c + width, :], preferred_element_type=F32)
            acc = term if acc is None else acc + term
        numer, denom = acc[:, :HD], acc[:, HD:]
        if has_state:
            shrink = jnp.exp2((old - peak) * F32(SCALE2))
            numer = numer + before[:, :HD] * shrink
            denom = denom + before[:, HD : HD + 1] * shrink
        if final:
            out_ref[r0 : r0 + q_rows, :] = (numer / denom).astype(BF16)
        else:
            lane = lax.broadcasted_iota(jnp.int32, (q_rows, HD), 1)
            out_ref[r0 : r0 + q_rows, :HD] = numer
            out_ref[r0 : r0 + q_rows, HD:] = jnp.where(lane < HD // 2, denom, peak)


def stage(flags, queries, pieces, state, final, name, q_rows=128, key_cols=512):
    rows, width = queries.shape
    heads = width // HD
    kinds = [p[0] for p in pieces]
    sizes = [p[1].shape[0] for p in pieces]
    total = sum(sizes)
    specs = [pl.BlockSpec(memory_space=pltpu.SMEM), pl.BlockSpec((rows, HD), lambda h: (0, h))]
    args = [flags, queries]
    for _, first, second in pieces:
        for a in (first, second):
            specs.append(pl.BlockSpec((a.shape[0], HD), lambda h: (0, h)))
            args.append(a)
    if state is not None:
        specs.append(pl.BlockSpec((rows, 2 * HD), lambda h: (0, h)))
        args.append(state)
    out = (
        jax.ShapeDtypeStruct((rows, width), BF16)
        if final
        else jax.ShapeDtypeStruct((rows, 2 * width), F32)
    )
    return pl.pallas_call(
        functools.partial(
            stage_body, kinds, sizes, state is not None, final, min(q_rows, rows), key_cols
        ),
        grid=(heads,),
        in_specs=specs,
        out_specs=pl.BlockSpec((rows, HD if final else 2 * HD), lambda h: (0, h)),
        out_shape=out,
        scratch_shapes=[
            pltpu.VMEM((total, HD), BF16),
            pltpu.VMEM((total, 2 * HD), BF16),
            pltpu.VMEM((2, min(q_rows, rows), total), F32),
        ],
        compiler_params=pltpu.CompilerParams(vmem_limit_bytes=40 * 2**20),
        cost_estimate=pl.CostEstimate(
            flops=rows * total * heads,
            bytes_accessed=rows * HD,
            transcendentals=0,
        ),
        name=name,
    )(*args)


def pooling(out_rows, in_rows, group, offset=0):
    r = lax.broadcasted_iota(jnp.int32, (out_rows, in_rows), 0)
    c = lax.broadcasted_iota(jnp.int32, (out_rows, in_rows), 1)
    return (r - offset == c // group).astype(BF16)


def mm(a, b):
    return jnp.dot(a, b, preferred_element_type=F32)


def on_device(queries, keys, values):
    tok, width = queries.shape
    count = lax.axis_size("ctx")
    depths = count.bit_length() - 1
    pos = lax.axis_index("ctx")
    odd = pos % 2 == 1

    def swap(x, bit):
        return lax.ppermute(x, "ctx", [(i, i ^ 2**bit) for i in range(count)])

    up = [(i, i + 1) for i in range(count - 1)]
    down = [(i + 1, i) for i in range(count - 1)]
    flags = jnp.stack([pos % 2, (pos > 0).astype(jnp.int32), (pos < count - 1).astype(jnp.int32)])
    flags = flags.astype(jnp.int32)

    group = tok // POOL
    m0 = pooling(POOL, tok, group)
    k0 = (mm(m0, keys) / F32(group**0.5)).astype(BF16)
    v0 = (mm(m0, values) / F32(group**0.5)).astype(BF16)
    sib_k0, sib_v0 = swap(k0, 0), swap(v0, 0)
    levels = [("plain", sib_k0, sib_v0)]
    mine = jnp.where(odd, v0, k0)
    partner = jnp.where(odd, sib_v0, sib_k0)
    for depth in range(1, depths):
        upper = pos // 2 ** (depth - 1) % 2
        half = POOL // 2
        own_m = pooling(POOL, POOL, 2, upper * half)
        sib_m = pooling(POOL, POOL, 2, (1 - upper) * half)
        mine = ((mm(own_m, mine) + mm(sib_m, partner)) / F32(2**0.5)).astype(BF16)
        if depth == 1:
            ends = [x for a in (keys, values) for x in (a[tok - EDGE :], a[:EDGE])]
        if depth < 3:
            partner = swap(mine, depth)
        else:
            bit = pos // 2 ** (depth - 1) % 2
            near = swap(lax.dynamic_slice_in_dim(mine, bit * half, half, 0), depth)
            near, state = lax.optimization_barrier(
                (near, stage(flags, queries, [waiting], state, False, "tree"))
            )
            far = swap(near, depth - 1)
            low = jnp.where(bit == 1, far, near)
            high = jnp.where(bit == 1, near, far)
            partner = jnp.concatenate([low, high], axis=0)
        if depth == 1:
            left_k, left_v = lax.ppermute(ends[0], "ctx", up), lax.ppermute(ends[2], "ctx", up)
            right_k, right_v = lax.ppermute(ends[1], "ctx", down), lax.ppermute(ends[3], "ctx", down)
            sides = [("left", left_k, left_v), ("right", right_k, right_v)]
            state = stage(flags, queries, [("plain", keys, values)], None, False, "own")
            partner, state = lax.optimization_barrier((partner, state))
        elif depth == 2:
            state = stage(flags, queries, levels + [waiting], state, False, "near")
            state = stage(flags, queries, sides, state, False, "sides")
            partner, state = lax.optimization_barrier((partner, state))
        waiting = ("level", partner, swap(partner, 0))
    return stage(flags, queries, [waiting], state, True, "root")


def solution(mesh):
    return jax.shard_map(
        on_device,
        mesh=mesh,
        in_specs=(P("ctx", "head"), P("ctx", "head"), P("ctx", "head")),
        out_specs=P("ctx", "head"),
        check_vma=False,
    )
```

time: 685 us -> 252 us (0.37)
  local copies, waits for them, and re-layouts: 261 us -> 11.8 us
  Pallas kernels: 0 us -> 186 us
  waiting for transfers between devices: 179 us -> 17.1 us
  other arithmetic: 130 us -> 0.43 us
  matrix products: 62.8 us -> 15.8 us
  loops' own time: 31.7 us -> 0 us
    pallas_call x0 -> x5, Pallas kernels: none -> 186 us  [stage(): pl.pallas_call(functools.partial(stage_body, kinds, sizes, state is not N...]
    ppermute x6 -> x13, waiting for transfers between devices: 179 us -> 17.1 us  [the longest x9 17.1 us: swap(): return lax.ppermute(x, 'ctx', [(i, i ^ 2 ** bit) for i in range(count)])]
    slice x16 -> x2, local copies, waits for them, and re-layouts: 137 us -> 3.01 us  [on_device(): ends = [x for a in (keys, values) for x in (a[tok - EDGE:], a[:EDGE])]]
    reduce_sum x36 -> x0, other arithmetic: 80.1 us -> none  [the longest x4 53 us: pool_rows(): jnp.sum(grouped, axis=-2) / jnp.float32(group ** 0.5)]
    dynamic_slice x80 -> x0, local copies, waits for them, and re-layouts: 50 us -> none  [the longest x32 19.1 us: one_head(): blocks = lax.map(one_block, jnp.arange(block_count, dtype=jnp.int32))]
    dot_general x64 -> x8, matrix products: 62.8 us -> 15.8 us  [mm(): return jnp.dot(a, b, preferred_element_type=F32)]
    convert_element_type x3 -> x0, local copies, waits for them, and re-layouts: 31.8 us -> none  [pool_rows(): block.reshape(shape[:-2] + (shape[-2] // group, group, shape[-1]))]
    another operation x17 -> x0, loops' own time: 31.7 us -> none  [the longest x16 20.8 us: one_head(): blocks = lax.map(one_block, jnp.arange(block_count, dtype=jnp.int32))]
  transfers between devices with their start and end apart: 6 -> 13, of which waited for: 3 -> 3; matrix products, arithmetic and copies ran while one was open for 6% -> 6% of each run, Pallas kernels for 0% -> 59%
where the time goes in v1:
time: 252 us; the launch traced here: 251 us
  Pallas kernels  186 us (74%)
  starting transfers between devices  19.8 us (8%)
  waiting for transfers between devices  17.1 us (7%)
  matrix products  15.8 us (6%)
  local copies, waits for them, and re-layouts  11.8 us (5%)
    pallas_call x5, Pallas kernels, stage(): pl.pallas_call(functools.partial(stage_body, kinds, sizes, state is not N...  186 us
    ppermute x9, waiting for transfers between devices, swap(): return lax.ppermute(x, 'ctx', [(i, i ^ 2 ** bit) for i in range(count)])  17.1 us
    dot_general x8, matrix products, mm(): return jnp.dot(a, b, preferred_element_type=F32)  15.8 us
    ppermute x9, starting transfers between devices, swap(): return lax.ppermute(x, 'ctx', [(i, i ^ 2 ** bit) for i in range(count)])  10.7 us
    unnamed x14, local copies, waits for them, and re-layouts  8.76 us
  transfers between devices with their start and end apart: 13, of which 3 were waited for; matrix products, arithmetic and copies ran while one was open for 6% of the time, Pallas kernels for 59%

profile of v1, /device:TPU:0, one launch (start us, length us, event | category | flops | bytes accessed | tf_op | source)
XLA Modules:
  0.0 250.9 jit_solution(2912439210901548210)
XLA Ops:
  0.0 3.6 %fusion.4 = bf16[256,2048]{1,0:T(8,128)(2,1)S(1)} fusion(bf16[1024,2048]{1,0:T(8,128)(2,1)} %refs_3_.1, s32[1024]{0:T(1024)S(1)} %get-tuple-element.23, s32[1024]{0:T(1024)S(1)} %get-tuple-element.24, pred[1024]{0:T(1024)(128)(4,1)S(1)} %fusion.48), kind=kOutput, calls=%fused_computation.8 | convolution fusion | flops 1075314688 | bytes 5252096 | tf_op jit(solution)/shard_map/dot_general | solution.py:137
  4.2 2.3 fusion.5
  6.5 1.7 fusion.9
  9.3 1.6 fusion.2
  10.9 2.7 %collective-permute-start.2 = (bf16[256,2048]{1,0:T(8,128)(2,1)}, bf16[256,2048]{1,0:T(8,128)(2,1)S(1)}, u32[]{:S(2)}, u32[]{:S(2)}) collective-permute-start(bf16[256,2048]{1,0:T(8,128)(2,1)} %fusion.2), channel_id=1, source_target_pairs={{0,4},{2,6},{4,0},{6,2},{8,12},{10,14},{12,8},{14,10},{16,20},{18,... | collective-permute-start | bytes 3145736 | tf_op jit(solution)/shard_map/ppermute | solution.py:148
  15.0 3.0 %collective-permute-start.4 = (bf16[256,2048]{1,0:T(8,128)(2,1)}, bf16[256,2048]{1,0:T(8,128)(2,1)}, u32[]{:S(2)}, u32[]{:S(2)}) collective-permute-start(bf16[256,2048]{1,0:T(8,128)(2,1)} %get-tuple-element.20), channel_id=1, source_target_pairs={{0,2},{2,4},{4,6},{6,8},{8,10},{10,12},{12,14},{14,16},{16,18},{18... | collective-permute-start | bytes 3145736 | tf_op jit(solution)/shard_map/ppermute | solution.py:184
  18.0 2.2 copy-done
  20.2 2.2 copy-done.5
  22.4 2.2 copy-done.6
  24.6 31.0 %own.1.refs_6_ = f32[1024,4096]{1,0:T(8,128)} custom-call(s32[3]{0:T(128)S(1)} %pad_add_fusion.refs_0_, bf16[1024,2048]{1,0:T(8,128)(2,1)S(1)} %copy-done, bf16[1024,2048]{1,0:T(8,128)(2,1)S(1)} %copy-done.5, bf16[1024,2048]{1,0:T(8,128)(2,1)S(1)} %copy-done.6), custom_call_target="tpu_custom_call" | custom-call | flops 16777216 | bytes 131072 | tf_op jit(solution)/shard_map/own/pallas_call | solution.py:107
  55.7 1.6 fusion.49
  57.2 3.4 %collective-permute-start.5 = (bf16[256,2048]{1,0:T(8,128)(2,1)}, bf16[256,2048]{1,0:T(8,128)(2,1)}, u32[]{:S(2)}, u32[]{:S(2)}) collective-permute-start(bf16[256,2048]{1,0:T(8,128)(2,1)} %get-tuple-element.18), channel_id=1, source_target_pairs={{0,2},{2,4},{4,6},{6,8},{8,10},{10,12},{12,14},{14,16},{16,18},{18... | collective-permute-start | bytes 3145736 | tf_op jit(solution)/shard_map/ppermute | solution.py:184
  63.4 1.7 fusion.20
  66.6 4.0 %collective-permute-start.3 = (bf16[256,2048]{1,0:T(8,128)(2,1)}, bf16[256,2048]{1,0:T(8,128)(2,1)}, u32[]{:S(2)}, u32[]{:S(2)}) collective-permute-start(bf16[256,2048]{1,0:T(8,128)(2,1)} %fusion.3), channel_id=1, source_target_pairs={{0,8},{2,10},{4,12},{6,14},{8,0},{10,2},{12,4},{14,6},{16,24},{18,... | collective-permute-start | bytes 3145736 | tf_op jit(solution)/shard_map/ppermute | solution.py:148
  70.7 1.7 fusion.19
  72.4 2.2 copy-done.1
  74.6 40.7 %near.1.refs_6_ = f32[1024,4096]{1,0:T(8,128)} custom-call(s32[3]{0:T(128)S(1)} %pad_add_fusion.refs_0_, bf16[1024,2048]{1,0:T(8,128)(2,1)S(1)} %copy-done.1, bf16[256,2048]{1,0:T(8,128)(2,1)S(1)} %collective-permute-done.1.refs_2_, bf16[256,2048]{1,0:T(8,128)(2,1)S(1)} %collective-permute-done.refs_3_, ...), custom_call_target="tpu_custom_call" | custom-call | flops 8388608 | bytes 131072 | tf_op jit(solution)/shard_map/near/pallas_call | solution.py:107
  115.3 39.9 %sides.1.refs_4_ = f32[1024,4096]{1,0:T(8,128)} custom-call(s32[3]{0:T(128)S(1)} %pad_add_fusion.refs_0_, bf16[1024,2048]{1,0:T(8,128)(2,1)S(1)} %copy-done.1, bf16[256,2048]{1,0:T(8,128)(2,1)} %collective-permute-done.4.refs_2_, bf16[256,2048]{1,0:T(8,128)(2,1)} %collective-permute-done.5.refs_3_, bf16[256,2048]{1,0:T(8,128)(2,1)} %collective-permute-done.6.refs_4_, ...), custom_call_target="tpu_custom_call" | custom-call | flops 8388608 | bytes 131072 | tf_op jit(solution)/shard_map/sides/pallas_call | solution.py:107
  155.4 1.7 fusion.21
  157.2 2.7 %collective-permute-start.9 = (bf16[128,2048]{1,0:T(8,128)(2,1)S(1)}, bf16[128,2048]{1,0:T(8,128)(2,1)S(1)}, u32[]{:S(2)}, u32[]{:S(2)}) collective-permute-start(bf16[128,2048]{1,0:T(8,128)(2,1)S(1)} %fusion.7), channel_id=1, source_target_pairs={{0,16},{2,18},{4,20},{6,22},{8,24},{10,26},{12,28},{14,30},{16,0},... | collective-permute-start | bytes 1572872 | tf_op jit(solution)/shard_map/ppermute | solution.py:148
  159.9 36.4 %tree.1.refs_4_ = f32[1024,4096]{1,0:T(8,128)} custom-call(s32[3]{0:T(128)S(1)} %pad_add_fusion.refs_0_, bf16[1024,2048]{1,0:T(8,128)(2,1)S(1)} %copy-done.1, bf16[256,2048]{1,0:T(8,128)(2,1)} %collective-permute-done.3.refs_2_, bf16[256,2048]{1,0:T(8,128)(2,1)S(1)} %collective-permute-done.10.refs_3_, f32[1024,4096]{1,0:T(8,128)} %sides.1.refs_4_), custom_call_target="tpu_custom_call" | custom-call | flops 4194304 | bytes 131072 | tf_op jit(solution)/shard_map/tree/pallas_call | solution.py:107
  196.7 13.4 %collective-permute-done.11 = bf16[128,2048]{1,0:T(8,128)(2,1)S(1)} collective-permute-done((bf16[128,2048]{1,0:T(8,128)(2,1)S(1)}, bf16[128,2048]{1,0:T(8,128)(2,1)S(1)}, u32[]{:S(2)}, u32[]{:S(2)}) %collective-permute-start.11) | collective-permute-done | bytes 524320 | tf_op jit(solution)/shard_map/ppermute | solution.py:148
  210.4 2.6 %collective-permute-done.12.refs_3_ = bf16[256,2048]{1,0:T(8,128)(2,1)S(1)} collective-permute-done((bf16[256,2048]{1,0:T(8,128)(2,1)S(1)}, bf16[256,2048]{1,0:T(8,128)(2,1)S(1)}, u32[]{:S(2)}, u32[]{:S(2)}) %collective-permute-start.12) | collective-permute-done | bytes 1048608 | tf_op jit(solution)/shard_map/ppermute | solution.py:148
  213.0 37.9 %root.1 = bf16[1024,2048]{1,0:T(8,128)(2,1)} custom-call(s32[3]{0:T(128)S(1)} %pad_add_fusion.refs_0_, bf16[1024,2048]{1,0:T(8,128)(2,1)S(1)} %copy-done.2, bf16[256,2048]{1,0:T(8,128)(2,1)S(1)} %pad_maximum_fusion.refs_2_, bf16[256,2048]{1,0:T(8,128)(2,1)S(1)} %collective-permute-done.12.refs_3_, f32[1024,4096]{1,0:T(8,128)} %tree.1.refs_4_), custom_call_target="tpu_custom_call" | custom-call | flops 4194304 | bytes 131072 | tf_op jit(solution)/shard_map/root/pallas_call | solution.py:107
  (44 shorter events, 8.5 us)
Async XLA Ops:
  0.0 4.1 %copy-start.3 = (bf16[1024,2048]{1,0:T(8,128)(2,1)S(1)}, bf16[1024,2048]{1,0:T(8,128)(2,1)}, u32[]{:S(2)}) copy-start(bf16[1024,2048]{1,0:T(8,128)(2,1)} %refs_2_.1) | copy-start | bytes 12582916
  3.6 4.6 %collective-permute-start = (bf16[256,2048]{1,0:T(8,128)(2,1)S(1)}, bf16[256,2048]{1,0:T(8,128)(2,1)S(1)}, u32[]{:S(2)}, u32[]{:S(2)}) collective-permute-start(bf16[256,2048]{1,0:T(8,128)(2,1)S(1)} %fusion.4), channel_id=1, source_target_pairs={{0,2},{2,0},{4,6},{6,4},{8,10},{10,8},{12,14},{14,12},{16,18},{18,... | collective-permute-start | bytes 3145736 | tf_op jit(solution)/shard_map/ppermute | solution.py:148
  6.4 2.9 %collective-permute-start.1 = (bf16[256,2048]{1,0:T(8,128)(2,1)}, bf16[256,2048]{1,0:T(8,128)(2,1)S(1)}, u32[]{:S(2)}, u32[]{:S(2)}) collective-permute-start(bf16[256,2048]{1,0:T(8,128)(2,1)} %fusion.5), channel_id=1, source_target_pairs={{0,2},{2,0},{4,6},{6,4},{8,10},{10,8},{12,14},{14,12},{16,18},{18,... | collective-permute-start | bytes 3145736 | tf_op jit(solution)/shard_map/ppermute | solution.py:148
  9.3 4.2 %copy-start.4 = (bf16[1024,2048]{1,0:T(8,128)(2,1)S(1)}, bf16[1024,2048]{1,0:T(8,128)(2,1)}, u32[]{:S(2)}) copy-start(bf16[1024,2048]{1,0:T(8,128)(2,1)} %refs_2_.1) | copy-start | bytes 12582916
  10.9 44.7 %collective-permute-start.2 = (bf16[256,2048]{1,0:T(8,128)(2,1)}, bf16[256,2048]{1,0:T(8,128)(2,1)S(1)}, u32[]{:S(2)}, u32[]{:S(2)}) collective-permute-start(bf16[256,2048]{1,0:T(8,128)(2,1)} %fusion.2), channel_id=1, source_target_pairs={{0,4},{2,6},{4,0},{6,2},{8,12},{10,14},{12,8},{14,10},{16,20},{18,... | collective-permute-start | bytes 3145736 | tf_op jit(solution)/shard_map/ppermute | solution.py:148
  15.0 100.3 %collective-permute-start.4 = (bf16[256,2048]{1,0:T(8,128)(2,1)}, bf16[256,2048]{1,0:T(8,128)(2,1)}, u32[]{:S(2)}, u32[]{:S(2)}) collective-permute-start(bf16[256,2048]{1,0:T(8,128)(2,1)} %get-tuple-element.20), channel_id=1, source_target_pairs={{0,2},{2,4},{4,6},{6,8},{8,10},{10,12},{12,14},{14,16},{16,18},{18... | collective-permute-start | bytes 3145736 | tf_op jit(solution)/shard_map/ppermute | solution.py:184
  18.0 2.2 copy-start
  20.2 2.2 copy-start.5
  22.4 2.2 copy-start.6
  55.6 11.0 %collective-permute-start.8 = (bf16[256,2048]{1,0:T(8,128)(2,1)S(1)}, bf16[256,2048]{1,0:T(8,128)(2,1)}, u32[]{:S(2)}, u32[]{:S(2)}) collective-permute-start(bf16[256,2048]{1,0:T(8,128)(2,1)S(1)} %collective-permute-done.2.refs_4_), channel_id=1, source_target_pairs={{0,2},{2,0},{4,6},{6,4},{8,10},{10,8},{12,14},{14,12},{16,18},{18,... | collective-permute-start | bytes 3145736 | tf_op jit(solution)/shard_map/ppermute | solution.py:148
  57.2 58.0 %collective-permute-start.5 = (bf16[256,2048]{1,0:T(8,128)(2,1)}, bf16[256,2048]{1,0:T(8,128)(2,1)}, u32[]{:S(2)}, u32[]{:S(2)}) collective-permute-start(bf16[256,2048]{1,0:T(8,128)(2,1)} %get-tuple-element.18), channel_id=1, source_target_pairs={{0,2},{2,4},{4,6},{6,8},{8,10},{10,12},{12,14},{14,16},{16,18},{18... | collective-permute-start | bytes 3145736 | tf_op jit(solution)/shard_map/ppermute | solution.py:184
  60.6 54.7 %collective-permute-start.6 = (bf16[256,2048]{1,0:T(8,128)(2,1)}, bf16[256,2048]{1,0:T(8,128)(2,1)}, u32[]{:S(2)}, u32[]{:S(2)}) collective-permute-start(bf16[256,2048]{1,0:T(8,128)(2,1)} %get-tuple-element.19), channel_id=1, source_target_pairs={{2,0},{4,2},{6,4},{8,6},{10,8},{12,10},{14,12},{16,14},{18,16},{20... | collective-permute-start | bytes 3145736 | tf_op jit(solution)/shard_map/ppermute | solution.py:185
  61.9 53.4 %collective-permute-start.7 = (bf16[256,2048]{1,0:T(8,128)(2,1)}, bf16[256,2048]{1,0:T(8,128)(2,1)}, u32[]{:S(2)}, u32[]{:S(2)}) collective-permute-start(bf16[256,2048]{1,0:T(8,128)(2,1)} %get-tuple-element.17), channel_id=1, source_target_pairs={{2,0},{4,2},{6,4},{8,6},{10,8},{12,10},{14,12},{16,14},{18,16},{20... | collective-permute-start | bytes 3145736 | tf_op jit(solution)/shard_map/ppermute | solution.py:185
  66.6 88.5 %collective-permute-start.3 = (bf16[256,2048]{1,0:T(8,128)(2,1)}, bf16[256,2048]{1,0:T(8,128)(2,1)}, u32[]{:S(2)}, u32[]{:S(2)}) collective-permute-start(bf16[256,2048]{1,0:T(8,128)(2,1)} %fusion.3), channel_id=1, source_target_pairs={{0,8},{2,10},{4,12},{6,14},{8,0},{10,2},{12,4},{14,6},{16,24},{18,... | collective-permute-start | bytes 3145736 | tf_op jit(solution)/shard_map/ppermute | solution.py:148
  72.4 2.2 copy-start.1
  155.2 4.7 %collective-permute-start.10 = (bf16[256,2048]{1,0:T(8,128)(2,1)}, bf16[256,2048]{1,0:T(8,128)(2,1)S(1)}, u32[]{:S(2)}, u32[]{:S(2)}) collective-permute-start(bf16[256,2048]{1,0:T(8,128)(2,1)} %collective-permute-done.3.refs_2_), channel_id=1, source_target_pairs={{0,2},{2,0},{4,6},{6,4},{8,10},{10,8},{12,14},{14,12},{16,18},{18,... | collective-permute-start | bytes 3145736 | tf_op jit(solution)/shard_map/ppermute | solution.py:148
  157.2 39.1 %collective-permute-start.9 = (bf16[128,2048]{1,0:T(8,128)(2,1)S(1)}, bf16[128,2048]{1,0:T(8,128)(2,1)S(1)}, u32[]{:S(2)}, u32[]{:S(2)}) collective-permute-start(bf16[128,2048]{1,0:T(8,128)(2,1)S(1)} %fusion.7), channel_id=1, source_target_pairs={{0,16},{2,18},{4,20},{6,22},{8,24},{10,26},{12,28},{14,30},{16,0},... | collective-permute-start | bytes 1572872 | tf_op jit(solution)/shard_map/ppermute | solution.py:148
  196.3 13.8 %collective-permute-start.11 = (bf16[128,2048]{1,0:T(8,128)(2,1)S(1)}, bf16[128,2048]{1,0:T(8,128)(2,1)S(1)}, u32[]{:S(2)}, u32[]{:S(2)}) collective-permute-start(bf16[128,2048]{1,0:T(8,128)(2,1)S(1)} %collective-permute-done.9), channel_id=1, source_target_pairs={{0,8},{2,10},{4,12},{6,14},{8,0},{10,2},{12,4},{14,6},{16,24},{18,... | collective-permute-start | bytes 1572872 | tf_op jit(solution)/shard_map/ppermute | solution.py:148
  196.7 16.3 %copy-start.2 = (bf16[1024,2048]{1,0:T(8,128)(2,1)S(1)}, bf16[1024,2048]{1,0:T(8,128)(2,1)}, u32[]{:S(2)}) copy-start(bf16[1024,2048]{1,0:T(8,128)(2,1)} %refs_1_.9) | copy-start | bytes 12582916
  210.3 2.7 %collective-permute-start.12 = (bf16[256,2048]{1,0:T(8,128)(2,1)S(1)}, bf16[256,2048]{1,0:T(8,128)(2,1)S(1)}, u32[]{:S(2)}, u32[]{:S(2)}) collective-permute-start(bf16[256,2048]{1,0:T(8,128)(2,1)S(1)} %pad_maximum_fusion.refs_2_), channel_id=1, source_target_pairs={{0,2},{2,0},{4,6},{6,4},{8,10},{10,8},{12,14},{14,12},{16,18},{18,... | collective-permute-start | bytes 3145736 | tf_op jit(solution)/shard_map/ppermute | solution.py:148

commit v2 on v1

--- a/solution.py
+++ b/solution.py
@@ -61,27 +61,28 @@
             for j in range(0, width, HD):
                 part = s[:, j : j + HD]
                 peak = part if peak is None else jnp.maximum(peak, part)
-        peak = jnp.max(peak, axis=-1, keepdims=True)
+        peak = jnp.broadcast_to(jnp.max(peak, axis=-1, keepdims=True), (q_rows, HD))
         if has_state:
             before = state_ref[r0 : r0 + q_rows, :]
-            old = before[:, 2 * HD - 1 :]
+            old = before[:, 2 * HD :]
             peak = jnp.maximum(peak, old)
         acc = None
         for c, width, flag in spans:
-            p = jnp.exp2((s_all[slot, :, c : c + width] - peak) * F32(SCALE2)).astype(BF16)
+            wide = jnp.concatenate([peak] * (width // HD), axis=1)
+            p = jnp.exp2((s_all[slot, :, c : c + width] - wide) * F32(SCALE2)).astype(BF16)
             term = jnp.dot(p, v_all[c : c + width, :], preferred_element_type=F32)
             acc = term if acc is None else acc + term
         numer, denom = acc[:, :HD], acc[:, HD:]
         if has_state:
             shrink = jnp.exp2((old - peak) * F32(SCALE2))
             numer = numer + before[:, :HD] * shrink
-            denom = denom + before[:, HD : HD + 1] * shrink
+            denom = denom + before[:, HD : 2 * HD] * shrink
         if final:
             out_ref[r0 : r0 + q_rows, :] = (numer / denom).astype(BF16)
         else:
-            lane = lax.broadcasted_iota(jnp.int32, (q_rows, HD), 1)
             out_ref[r0 : r0 + q_rows, :HD] = numer
-            out_ref[r0 : r0 + q_rows, HD:] = jnp.where(lane < HD // 2, denom, peak)
+            out_ref[r0 : r0 + q_rows, HD : 2 * HD] = denom
+            out_ref[r0 : r0 + q_rows, 2 * HD :] = peak
 
 
 def stage(flags, queries, pieces, state, final, name, q_rows=128, key_cols=512):
@@ -97,12 +98,12 @@
             specs.append(pl.BlockSpec((a.shape[0], HD), lambda h: (0, h)))
             args.append(a)
     if state is not None:
-        specs.append(pl.BlockSpec((rows, 2 * HD), lambda h: (0, h)))
+        specs.append(pl.BlockSpec((rows, 3 * HD), lambda h: (0, h)))
         args.append(state)
     out = (
         jax.ShapeDtypeStruct((rows, width), BF16)
         if final
-        else jax.ShapeDtypeStruct((rows, 2 * width), F32)
+        else jax.ShapeDtypeStruct((rows, 3 * width), F32)
     )
     return pl.pallas_call(
         functools.partial(
@@ -110,7 +111,7 @@
         ),
         grid=(heads,),
         in_specs=specs,
-        out_specs=pl.BlockSpec((rows, HD if final else 2 * HD), lambda h: (0, h)),
+        out_specs=pl.BlockSpec((rows, HD if final else 3 * HD), lambda h: (0, h)),
         out_shape=out,
         scratch_shapes=[
             pltpu.VMEM((total, HD), BF16),
@@ -174,8 +175,9 @@
             bit = pos // 2 ** (depth - 1) % 2
             near = swap(lax.dynamic_slice_in_dim(mine, bit * half, half, 0), depth)
             near, state = lax.optimization_barrier(
-                (near, stage(flags, queries, [waiting], state, False, "tree"))
+                (near, stage(flags, queries, sides + [waiting], state, False, "tree"))
             )
+            sides = []
             far = swap(near, depth - 1)
             low = jnp.where(bit == 1, far, near)
             high = jnp.where(bit == 1, near, far)
@@ -188,7 +190,6 @@
             partner, state = lax.optimization_barrier((partner, state))
         elif depth == 2:
             state = stage(flags, queries, levels + [waiting], state, False, "near")
-            state = stage(flags, queries, sides, state, False, "sides")
             partner, state = lax.optimization_barrier((partner, state))
         waiting = ("level", partner, swap(partner, 0))
     return stage(flags, queries, [waiting], state, True, "root")

time: 252 us -> 173 us (0.69)
  Pallas kernels: 186 us -> 108 us
  matrix products: 15.8 us -> 12.5 us
  waiting for transfers between devices: 17.1 us -> 14.5 us
  starting transfers between devices: 19.8 us -> 22.4 us
    pallas_call x5 -> x4, Pallas kernels: 186 us -> 108 us  [stage(): pl.pallas_call(functools.partial(stage_body, kinds, sizes, state is not N...]
    ppermute x9, starting transfers between devices: 10.7 us -> 14 us  [swap(): return lax.ppermute(x, 'ctx', [(i, i ^ 2 ** bit) for i in range(count)])]
    dot_general x8, matrix products: 15.8 us -> 12.5 us  [mm(): return jnp.dot(a, b, preferred_element_type=F32)]
    ppermute x9, waiting for transfers between devices: 17.1 us -> 14.5 us  [swap(): return lax.ppermute(x, 'ctx', [(i, i ^ 2 ** bit) for i in range(count)])]
    unnamed x14 -> x20, local copies, waits for them, and re-layouts: 8.76 us -> 9.77 us
  transfers between devices with their start and end apart: 13 -> 13, of which waited for: 3 -> 3; matrix products, arithmetic and copies ran while one was open for 6% -> 7% of each run, Pallas kernels for 59% -> 52%
where the time goes in v2:
time: 173 us; the launch traced here: 171 us
  Pallas kernels  108 us (62%)
  starting transfers between devices  22.4 us (13%)
  waiting for transfers between devices  14.5 us (8%)
  local copies, waits for them, and re-layouts  12.8 us (7%)
  matrix products  12.5 us (7%)
    pallas_call x4, Pallas kernels, stage(): pl.pallas_call(functools.partial(stage_body, kinds, sizes, state is not N...  108 us
    ppermute x9, waiting for transfers between devices, swap(): return lax.ppermute(x, 'ctx', [(i, i ^ 2 ** bit) for i in range(count)])  14.5 us
    ppermute x9, starting transfers between devices, swap(): return lax.ppermute(x, 'ctx', [(i, i ^ 2 ** bit) for i in range(count)])  14 us
    dot_general x8, matrix products, mm(): return jnp.dot(a, b, preferred_element_type=F32)  12.5 us
    unnamed x20, local copies, waits for them, and re-layouts  9.77 us
  transfers between devices with their start and end apart: 13, of which 3 were waited for; matrix products, arithmetic and copies ran while one was open for 7% of the time, Pallas kernels for 52%

profile of v2, /device:TPU:0, one launch (start us, length us, event | category | flops | bytes accessed | tf_op | source)
XLA Modules:
  0.0 171.2 jit_solution(964477908937068976)
XLA Ops:
  0.0 3.6 %fusion.4 = bf16[256,2048]{1,0:T(8,128)(2,1)S(1)} fusion(bf16[1024,2048]{1,0:T(8,128)(2,1)} %refs_3_.1, s32[1024]{0:T(1024)S(1)} %get-tuple-element.23, s32[1024]{0:T(1024)S(1)} %get-tuple-element.24, pred[1024]{0:T(1024)(128)(4,1)S(1)} %fusion.48), kind=kOutput, calls=%fused_computation.8 | convolution fusion | flops 1075314688 | bytes 5252096 | tf_op jit(solution)/shard_map/dot_general | solution.py:138
  4.2 2.3 %fusion.5 = bf16[256,2048]{1,0:T(8,128)(2,1)} fusion(bf16[1024,2048]{1,0:T(8,128)(2,1)S(1)} %copy-done.3, s32[1024]{0:T(1024)S(1)} %get-tuple-element.23, s32[1024]{0:T(1024)S(1)} %get-tuple-element.24, pred[1024]{0:T(1024)(128)(4,1)S(1)} %fusion.48), kind=kOutput, calls=%fused_computation.9 | convolution fusion | flops 1075314688 | bytes 5252096 | tf_op jit(solution)/shard_map/dot_general | solution.py:138
  6.5 1.7 fusion.9
  10.9 2.7 %collective-permute-start.2 = (bf16[256,2048]{1,0:T(8,128)(2,1)S(1)}, bf16[256,2048]{1,0:T(8,128)(2,1)S(1)}, u32[]{:S(2)}, u32[]{:S(2)}) collective-permute-start(bf16[256,2048]{1,0:T(8,128)(2,1)S(1)} %fusion.2), channel_id=1, source_target_pairs={{0,4},{2,6},{4,0},{6,2},{8,12},{10,14},{12,8},{14,10},{16,20},{18,... | collective-permute-start | bytes 3145736 | tf_op jit(solution)/shard_map/ppermute | solution.py:149
  15.0 3.0 %collective-permute-start.6 = (bf16[256,2048]{1,0:T(8,128)(2,1)}, bf16[256,2048]{1,0:T(8,128)(2,1)}, u32[]{:S(2)}, u32[]{:S(2)}) collective-permute-start(bf16[256,2048]{1,0:T(8,128)(2,1)} %get-tuple-element.20), channel_id=1, source_target_pairs={{0,2},{2,4},{4,6},{6,8},{8,10},{10,12},{12,14},{14,16},{16,18},{18... | collective-permute-start | bytes 3145736 | tf_op jit(solution)/shard_map/ppermute | solution.py:186
  18.1 2.2 %copy-done = bf16[1024,2048]{1,0:T(8,128)(2,1)S(1)} copy-done((bf16[1024,2048]{1,0:T(8,128)(2,1)S(1)}, bf16[1024,2048]{1,0:T(8,128)(2,1)}, u32[]{:S(2)}) %copy-start) | copy-done | bytes 4194328
  20.3 2.2 %copy-done.5 = bf16[1024,2048]{1,0:T(8,128)(2,1)S(1)} copy-done((bf16[1024,2048]{1,0:T(8,128)(2,1)S(1)}, bf16[1024,2048]{1,0:T(8,128)(2,1)}, u32[]{:S(2)}) %copy-start.5) | copy-done | bytes 4194328
  22.4 2.2 %copy-done.6 = bf16[1024,2048]{1,0:T(8,128)(2,1)S(1)} copy-done((bf16[1024,2048]{1,0:T(8,128)(2,1)S(1)}, bf16[1024,2048]{1,0:T(8,128)(2,1)}, u32[]{:S(2)}) %copy-start.6) | copy-done | bytes 4194328
  24.6 31.4 %own.1.refs_6_ = f32[1024,6144]{1,0:T(8,128)} custom-call(s32[3]{0:T(128)S(1)} %pad_add_fusion.refs_0_, bf16[1024,2048]{1,0:T(8,128)(2,1)S(1)} %copy-done, bf16[1024,2048]{1,0:T(8,128)(2,1)S(1)} %copy-done.5, bf16[1024,2048]{1,0:T(8,128)(2,1)S(1)} %copy-done.6), custom_call_target="tpu_custom_call" | custom-call | flops 16777216 | bytes 131072 | tf_op jit(solution)/shard_map/own/pallas_call | solution.py:108
  56.6 1.5 fusion.3
  58.1 1.6 collective-permute-start.3
  59.7 1.6 fusion.49
  61.2 2.7 %collective-permute-start.7 = (bf16[256,2048]{1,0:T(8,128)(2,1)}, bf16[256,2048]{1,0:T(8,128)(2,1)}, u32[]{:S(2)}, u32[]{:S(2)}) collective-permute-start(bf16[256,2048]{1,0:T(8,128)(2,1)} %get-tuple-element.18), channel_id=1, source_target_pairs={{0,2},{2,4},{4,6},{6,8},{8,10},{10,12},{12,14},{14,16},{16,18},{18... | collective-permute-start | bytes 3145736 | tf_op jit(solution)/shard_map/ppermute | solution.py:186
  65.3 1.9 %fusion.19 = f32[256,2048]{1,0:T(8,128)S(1)} fusion(bf16[256,2048]{1,0:T(8,128)(2,1)} %fusion.3, s32[256]{0:T(256)S(1)} %get-tuple-element.25, s32[256]{0:T(256)S(1)} %get-tuple-element.28, s32[256]{0:T(256)S(1)} %iota_subtract_fusion.5, pred[256]{0:T(512)(128)(4,1)S(1)} %compare_and_fusion), kind=kOutput, calls=%fused_computation.34 | convolution fusion | flops 268566528 | bytes 3149056 | tf_op jit(solution)/shard_map/dot_general | solution.py:138
  67.1 1.5 collective-permute-start.9
  68.6 2.2 %copy-done.1 = bf16[1024,2048]{1,0:T(8,128)(2,1)S(1)} copy-done((bf16[1024,2048]{1,0:T(8,128)(2,1)S(1)}, bf16[1024,2048]{1,0:T(8,128)(2,1)}, u32[]{:S(2)}) %copy-start.1) | copy-done | bytes 4194328
  70.8 26.7 %near.1.refs_8_ = f32[1024,6144]{1,0:T(8,128)} custom-call(s32[3]{0:T(128)S(1)} %pad_add_fusion.refs_0_, bf16[1024,2048]{1,0:T(8,128)(2,1)S(1)} %copy-done.1, bf16[256,2048]{1,0:T(8,128)(2,1)S(1)} %copy-done.8, bf16[256,2048]{1,0:T(8,128)(2,1)S(1)} %collective-permute-done.refs_3_, bf16[256,2048]{1,0:T(8,128)(2,1)S(1)} %collective-permute-done.2.refs_4_, ...), custom_call_target="tpu_custom_call" | custom-call | flops 8388608 | bytes 131072 | tf_op jit(solution)/shard_map/near/pallas_call | solution.py:108
  97.5 2.7 %collective-permute-start.10 = (bf16[256,2048]{1,0:T(8,128)(2,1)S(1)}, bf16[256,2048]{1,0:T(8,128)(2,1)S(1)}, u32[]{:S(2)}, u32[]{:S(2)}) collective-permute-start(bf16[256,2048]{1,0:T(8,128)(2,1)S(1)} %collective-permute-done.3.refs_6_), channel_id=1, source_target_pairs={{0,2},{2,0},{4,6},{6,4},{8,10},{10,8},{12,14},{14,12},{16,18},{18,... | collective-permute-start | bytes 3145736 | tf_op jit(solution)/shard_map/ppermute | solution.py:149
  100.9 3.6 %collective-permute-start.5 = (bf16[128,2048]{1,0:T(8,128)(2,1)S(1)}, bf16[128,2048]{1,0:T(8,128)(2,1)S(1)}, u32[]{:S(2)}, u32[]{:S(2)}) collective-permute-start(bf16[128,2048]{1,0:T(8,128)(2,1)S(1)} %fusion.7), channel_id=1, source_target_pairs={{0,16},{2,18},{4,20},{6,22},{8,24},{10,26},{12,28},{14,30},{16,0},... | collective-permute-start | bytes 1572872 | tf_op jit(solution)/shard_map/ppermute | solution.py:149
  104.5 30.4 %tree.1.refs_4_ = f32[1024,6144]{1,0:T(8,128)} custom-call(s32[3]{0:T(128)S(1)} %pad_add_fusion.refs_0_, bf16[1024,2048]{1,0:T(8,128)(2,1)S(1)} %copy-done.1, bf16[256,2048]{1,0:T(8,128)(2,1)} %collective-permute-done.6.refs_2_, bf16[256,2048]{1,0:T(8,128)(2,1)} %collective-permute-done.7.refs_3_, bf16[256,2048]{1,0:T(8,128)(2,1)} %collective-permute-done.8.refs_4_, ...), custom_call_target="tpu_custom_call" | custom-call | flops 12582912 | bytes 131072 | tf_op jit(solution)/shard_map/tree/pallas_call | solution.py:108
  134.9 2.8 %collective-permute-start.11 = (bf16[128,2048]{1,0:T(8,128)(2,1)S(1)}, bf16[128,2048]{1,0:T(8,128)(2,1)S(1)}, u32[]{:S(2)}, u32[]{:S(2)}) collective-permute-start(bf16[128,2048]{1,0:T(8,128)(2,1)S(1)} %collective-permute-done.5), channel_id=1, source_target_pairs={{0,8},{2,10},{4,12},{6,14},{8,0},{10,2},{12,4},{14,6},{16,24},{18,... | collective-permute-start | bytes 1572872 | tf_op jit(solution)/shard_map/ppermute | solution.py:149
  137.6 10.8 %collective-permute-done.11 = bf16[128,2048]{1,0:T(8,128)(2,1)S(1)} collective-permute-done((bf16[128,2048]{1,0:T(8,128)(2,1)S(1)}, bf16[128,2048]{1,0:T(8,128)(2,1)S(1)}, u32[]{:S(2)}, u32[]{:S(2)}) %collective-permute-start.11) | collective-permute-done | bytes 524320 | tf_op jit(solution)/shard_map/ppermute | solution.py:149
  148.7 2.6 %collective-permute-done.12.refs_3_ = bf16[256,2048]{1,0:T(8,128)(2,1)S(1)} collective-permute-done((bf16[256,2048]{1,0:T(8,128)(2,1)S(1)}, bf16[256,2048]{1,0:T(8,128)(2,1)S(1)}, u32[]{:S(2)}, u32[]{:S(2)}) %collective-permute-start.12) | collective-permute-done | bytes 1048608 | tf_op jit(solution)/shard_map/ppermute | solution.py:149
  151.3 19.9 %root.1 = bf16[1024,2048]{1,0:T(8,128)(2,1)} custom-call(s32[3]{0:T(128)S(1)} %pad_add_fusion.refs_0_, bf16[1024,2048]{1,0:T(8,128)(2,1)S(1)} %copy-done.2, bf16[256,2048]{1,0:T(8,128)(2,1)S(1)} %pad_maximum_fusion.refs_2_, bf16[256,2048]{1,0:T(8,128)(2,1)S(1)} %collective-permute-done.12.refs_3_, f32[1024,6144]{1,0:T(8,128)} %tree.1.refs_4_), custom_call_target="tpu_custom_call" | custom-call | flops 4194304 | bytes 131072 | tf_op jit(solution)/shard_map/root/pallas_call | solution.py:108
  (49 shorter events, 7.5 us)
Async XLA Ops:
  0.0 4.1 %copy-start.3 = (bf16[1024,2048]{1,0:T(8,128)(2,1)S(1)}, bf16[1024,2048]{1,0:T(8,128)(2,1)}, u32[]{:S(2)}) copy-start(bf16[1024,2048]{1,0:T(8,128)(2,1)} %refs_2_.1) | copy-start | bytes 12582916
  3.6 4.6 %collective-permute-start = (bf16[256,2048]{1,0:T(8,128)(2,1)S(1)}, bf16[256,2048]{1,0:T(8,128)(2,1)S(1)}, u32[]{:S(2)}, u32[]{:S(2)}) collective-permute-start(bf16[256,2048]{1,0:T(8,128)(2,1)S(1)} %fusion.4), channel_id=1, source_target_pairs={{0,2},{2,0},{4,6},{6,4},{8,10},{10,8},{12,14},{14,12},{16,18},{18,... | collective-permute-start | bytes 3145736 | tf_op jit(solution)/shard_map/ppermute | solution.py:149
  6.4 2.9 %collective-permute-start.1 = (bf16[256,2048]{1,0:T(8,128)(2,1)}, bf16[256,2048]{1,0:T(8,128)(2,1)S(1)}, u32[]{:S(2)}, u32[]{:S(2)}) collective-permute-start(bf16[256,2048]{1,0:T(8,128)(2,1)} %fusion.5), channel_id=1, source_target_pairs={{0,2},{2,0},{4,6},{6,4},{8,10},{10,8},{12,14},{14,12},{16,18},{18,... | collective-permute-start | bytes 3145736 | tf_op jit(solution)/shard_map/ppermute | solution.py:149
  9.3 4.3 %copy-start.4 = (bf16[1024,2048]{1,0:T(8,128)(2,1)S(1)}, bf16[1024,2048]{1,0:T(8,128)(2,1)}, u32[]{:S(2)}) copy-start(bf16[1024,2048]{1,0:T(8,128)(2,1)} %refs_2_.1) | copy-start | bytes 12582916
  9.9 1.0 copy-start.7
  10.9 45.6 %collective-permute-start.2 = (bf16[256,2048]{1,0:T(8,128)(2,1)S(1)}, bf16[256,2048]{1,0:T(8,128)(2,1)S(1)}, u32[]{:S(2)}, u32[]{:S(2)}) collective-permute-start(bf16[256,2048]{1,0:T(8,128)(2,1)S(1)} %fusion.2), channel_id=1, source_target_pairs={{0,4},{2,6},{4,0},{6,2},{8,12},{10,14},{12,8},{14,10},{16,20},{18,... | collective-permute-start | bytes 3145736 | tf_op jit(solution)/shard_map/ppermute | solution.py:149
  15.0 85.9 %collective-permute-start.6 = (bf16[256,2048]{1,0:T(8,128)(2,1)}, bf16[256,2048]{1,0:T(8,128)(2,1)}, u32[]{:S(2)}, u32[]{:S(2)}) collective-permute-start(bf16[256,2048]{1,0:T(8,128)(2,1)} %get-tuple-element.20), channel_id=1, source_target_pairs={{0,2},{2,4},{4,6},{6,8},{8,10},{10,12},{12,14},{14,16},{16,18},{18... | collective-permute-start | bytes 3145736 | tf_op jit(solution)/shard_map/ppermute | solution.py:186
  18.1 2.2 %copy-start = (bf16[1024,2048]{1,0:T(8,128)(2,1)S(1)}, bf16[1024,2048]{1,0:T(8,128)(2,1)}, u32[]{:S(2)}) copy-start(bf16[1024,2048]{1,0:T(8,128)(2,1)} %refs_1_.7) | copy-start | bytes 12582916
  20.3 2.2 %copy-start.5 = (bf16[1024,2048]{1,0:T(8,128)(2,1)S(1)}, bf16[1024,2048]{1,0:T(8,128)(2,1)}, u32[]{:S(2)}) copy-start(bf16[1024,2048]{1,0:T(8,128)(2,1)} %refs_2_.1) | copy-start | bytes 12582916
  22.4 2.2 %copy-start.6 = (bf16[1024,2048]{1,0:T(8,128)(2,1)S(1)}, bf16[1024,2048]{1,0:T(8,128)(2,1)}, u32[]{:S(2)}) copy-start(bf16[1024,2048]{1,0:T(8,128)(2,1)} %refs_3_.1) | copy-start | bytes 12582916
  56.5 10.6 %collective-permute-start.4 = (bf16[256,2048]{1,0:T(8,128)(2,1)S(1)}, bf16[256,2048]{1,0:T(8,128)(2,1)}, u32[]{:S(2)}, u32[]{:S(2)}) collective-permute-start(bf16[256,2048]{1,0:T(8,128)(2,1)S(1)} %collective-permute-done.2.refs_4_), channel_id=1, source_target_pairs={{0,2},{2,0},{4,6},{6,4},{8,10},{10,8},{12,14},{14,12},{16,18},{18,... | collective-permute-start | bytes 3145736 | tf_op jit(solution)/shard_map/ppermute | solution.py:149
  58.1 39.4 %collective-permute-start.3 = (bf16[256,2048]{1,0:T(8,128)(2,1)}, bf16[256,2048]{1,0:T(8,128)(2,1)S(1)}, u32[]{:S(2)}, u32[]{:S(2)}) collective-permute-start(bf16[256,2048]{1,0:T(8,128)(2,1)} %fusion.3), channel_id=1, source_target_pairs={{0,8},{2,10},{4,12},{6,14},{8,0},{10,2},{12,4},{14,6},{16,24},{18,... | collective-permute-start | bytes 3145736 | tf_op jit(solution)/shard_map/ppermute | solution.py:149
  61.2 43.3 %collective-permute-start.7 = (bf16[256,2048]{1,0:T(8,128)(2,1)}, bf16[256,2048]{1,0:T(8,128)(2,1)}, u32[]{:S(2)}, u32[]{:S(2)}) collective-permute-start(bf16[256,2048]{1,0:T(8,128)(2,1)} %get-tuple-element.18), channel_id=1, source_target_pairs={{0,2},{2,4},{4,6},{6,8},{8,10},{10,12},{12,14},{14,16},{16,18},{18... | collective-permute-start | bytes 3145736 | tf_op jit(solution)/shard_map/ppermute | solution.py:186
  63.9 40.6 %collective-permute-start.8 = (bf16[256,2048]{1,0:T(8,128)(2,1)}, bf16[256,2048]{1,0:T(8,128)(2,1)}, u32[]{:S(2)}, u32[]{:S(2)}) collective-permute-start(bf16[256,2048]{1,0:T(8,128)(2,1)} %get-tuple-element.19), channel_id=1, source_target_pairs={{2,0},{4,2},{6,4},{8,6},{10,8},{12,10},{14,12},{16,14},{18,16},{20... | collective-permute-start | bytes 3145736 | tf_op jit(solution)/shard_map/ppermute | solution.py:187
  65.2 1.9 %copy-start.9 = (bf16[256,2048]{1,0:T(8,128)(2,1)S(1)}, bf16[256,2048]{1,0:T(8,128)(2,1)}, u32[]{:S(2)}) copy-start(bf16[256,2048]{1,0:T(8,128)(2,1)} %get-tuple-element.17) | copy-start | bytes 3145732
  65.2 3.4 %copy-start.8 = (bf16[256,2048]{1,0:T(8,128)(2,1)S(1)}, bf16[256,2048]{1,0:T(8,128)(2,1)}, u32[]{:S(2)}) copy-start(bf16[256,2048]{1,0:T(8,128)(2,1)} %copy-done.7) | copy-start | bytes 3145732
  67.1 37.4 %collective-permute-start.9 = (bf16[256,2048]{1,0:T(8,128)(2,1)S(1)}, bf16[256,2048]{1,0:T(8,128)(2,1)S(1)}, u32[]{:S(2)}, u32[]{:S(2)}) collective-permute-start(bf16[256,2048]{1,0:T(8,128)(2,1)S(1)} %copy-done.9), channel_id=1, source_target_pairs={{2,0},{4,2},{6,4},{8,6},{10,8},{12,10},{14,12},{16,14},{18,16},{20... | collective-permute-start | bytes 3145736 | tf_op jit(solution)/shard_map/ppermute | solution.py:187
  68.6 2.2 %copy-start.1 = (bf16[1024,2048]{1,0:T(8,128)(2,1)S(1)}, bf16[1024,2048]{1,0:T(8,128)(2,1)}, u32[]{:S(2)}) copy-start(bf16[1024,2048]{1,0:T(8,128)(2,1)} %refs_1_.7) | copy-start | bytes 12582916
  97.5 7.0 %collective-permute-start.10 = (bf16[256,2048]{1,0:T(8,128)(2,1)S(1)}, bf16[256,2048]{1,0:T(8,128)(2,1)S(1)}, u32[]{:S(2)}, u32[]{:S(2)}) collective-permute-start(bf16[256,2048]{1,0:T(8,128)(2,1)S(1)} %collective-permute-done.3.refs_6_), channel_id=1, source_target_pairs={{0,2},{2,0},{4,6},{6,4},{8,10},{10,8},{12,14},{14,12},{16,18},{18,... | collective-permute-start | bytes 3145736 | tf_op jit(solution)/shard_map/ppermute | solution.py:149
  100.9 34.0 %collective-permute-start.5 = (bf16[128,2048]{1,0:T(8,128)(2,1)S(1)}, bf16[128,2048]{1,0:T(8,128)(2,1)S(1)}, u32[]{:S(2)}, u32[]{:S(2)}) collective-permute-start(bf16[128,2048]{1,0:T(8,128)(2,1)S(1)} %fusion.7), channel_id=1, source_target_pairs={{0,16},{2,18},{4,20},{6,22},{8,24},{10,26},{12,28},{14,30},{16,0},... | collective-permute-start | bytes 1572872 | tf_op jit(solution)/shard_map/ppermute | solution.py:149
  134.9 13.6 %collective-permute-start.11 = (bf16[128,2048]{1,0:T(8,128)(2,1)S(1)}, bf16[128,2048]{1,0:T(8,128)(2,1)S(1)}, u32[]{:S(2)}, u32[]{:S(2)}) collective-permute-start(bf16[128,2048]{1,0:T(8,128)(2,1)S(1)} %collective-permute-done.5), channel_id=1, source_target_pairs={{0,8},{2,10},{4,12},{6,14},{8,0},{10,2},{12,4},{14,6},{16,24},{18,... | collective-permute-start | bytes 1572872 | tf_op jit(solution)/shard_map/ppermute | solution.py:149
  137.6 13.7 %copy-start.2 = (bf16[1024,2048]{1,0:T(8,128)(2,1)S(1)}, bf16[1024,2048]{1,0:T(8,128)(2,1)}, u32[]{:S(2)}) copy-start(bf16[1024,2048]{1,0:T(8,128)(2,1)} %refs_1_.7) | copy-start | bytes 12582916
  148.6 2.7 %collective-permute-start.12 = (bf16[256,2048]{1,0:T(8,128)(2,1)S(1)}, bf16[256,2048]{1,0:T(8,128)(2,1)S(1)}, u32[]{:S(2)}, u32[]{:S(2)}) collective-permute-start(bf16[256,2048]{1,0:T(8,128)(2,1)S(1)} %pad_maximum_fusion.refs_2_), channel_id=1, source_target_pairs={{0,2},{2,0},{4,6},{6,4},{8,10},{10,8},{12,14},{14,12},{16,18},{18,... | collective-permute-start | bytes 3145736 | tf_op jit(solution)/shard_map/ppermute | solution.py:149
